TPU v7x, 256 devices: a whole 4x4x8 slice. The times are simulated.
256 devices in a mesh: site: 8 (over z), sector: 32 (over x, y, core).
Axes of the slice: x: 4, y: 4, z: 8, core: 2. Of those that a mesh axis runs over, the one named last changes fastest.
Arguments:
- initial_state: float32 [8, 32, 128, 128], P('site', 'sector')
- left_env: bfloat16 [8, 32, 4, 12, 128, 128], P('site', 'sector'), may hold values from -0.5 to 0.5
- edge_env: bfloat16 [32, 4, 12, 128, 128], P('sector'), may hold values from -0.5 to 0.5
- right_env: bfloat16 [8, 32, 4, 12, 128, 128], P('site', 'sector'), may hold values from -0.15625 to 0.15625
- source_blocks: int32 [8, 32, 4], P('site', 'sector'), may hold values from 0 to 31, as said below
- live_terms: int32 [8, 32], P('site', 'sector'), may hold values from 1 to 4
Outputs:
- state: float32 [8, 32, 128, 128], P('site', 'sector')
- energy: float32 [8], P('site')
Inputs may be any that keep to these rules, and one draw needn't show every extreme that they name: source_blocks[s, b, 0] = b; every other entry is b - 1, b + 1, b - 4 or b + 4.
All inputs are finite; a program needn't handle non-finite values.
Results may differ from a plain program's by a relative error of at most 0.015.
Values may be sent and summed in bfloat16 or wider, within the bound.
A program may use at most 64 MiB of HBM per device.

v0:
```python
import jax
import jax.numpy as jnp
from jax import lax
from jax.sharding import PartitionSpec as P

GRID = 4
ITERS = 8


def passed_along(x, axis, by):
    size = lax.axis_size(axis)
    pairs = [(i, i + by) for i in range(size) if 0 <= i + by < size]
    return lax.ppermute(x, axis, pairs)


def per_device(initial_state, left_env, edge_env, right_env, source_blocks, live_terms):
    width = initial_state.shape[-1]
    cells = lax.axis_size("sector") * width * width
    handed = passed_along(left_env, "site", 1)
    left_side = jnp.where(lax.axis_index("site") == 0, edge_env[0], handed[0, 0])
    right_side = right_env[0, 0]
    source_ids = source_blocks[0, 0]
    live_count = live_terms[0, 0]
    my_block = lax.axis_index("sector")

    def fetch(rounded):
        lower = passed_along(rounded, "sector", 1)
        upper = passed_along(rounded, "sector", -1)
        below = passed_along(rounded, "sector", GRID)
        above = passed_along(rounded, "sector", -GRID)
        stacked = jnp.concatenate([rounded[0], lower[0], upper[0], below[0], above[0]], 0)
        offset = source_ids - my_block
        slot = jnp.where(
            offset == 0,
            0,
            jnp.where(offset == -1, 1, jnp.where(offset == 1, 2, jnp.where(offset == -GRID, 3, 4))),
        )
        return jnp.take(stacked, slot, axis=0)

    def operate(vector):
        pieces = fetch(vector.astype(jnp.bfloat16))

        def add_term(j, total):
            left_block = lax.dynamic_index_in_dim(left_side, j, 0, keepdims=False)
            right_block = lax.dynamic_index_in_dim(right_side, j, 0, keepdims=False)
            piece = lax.dynamic_index_in_dim(pieces, j, 0, keepdims=False)
            product = jnp.einsum(
                "wlk,kr->wlr", left_block, piece, preferred_element_type=jnp.float32
            ).astype(jnp.bfloat16)
            return total + jnp.einsum(
                "wls,wsr->lr", product, right_block, preferred_element_type=jnp.float32
            )

        total = lax.fori_loop(0, live_count, add_term, jnp.zeros((width, width), jnp.float32))
        return total[None, None]

    start_norm = lax.psum(jnp.sum(initial_state * initial_state), "sector") / cells
    wave_now = initial_state / jnp.sqrt(start_norm + 1e-06)
    wave_image = operate(wave_now)
    energy = jnp.float32(0.0)
    rayleigh = jnp.float32(0.0)
    for step in range(ITERS):
        rayleigh = lax.psum(jnp.sum(wave_now * wave_image), "sector") / cells
        residual = wave_image - rayleigh * wave_now
        resid_norm = lax.psum(jnp.sum(residual * residual), "sector") / cells
        correction = residual / jnp.sqrt(resid_norm + 1e-06)
        corr_image = operate(correction)
        cross_one, cross_two, corr_sum, image_cross, corr_square = lax.psum(
            (
                jnp.sum(correction * wave_image),
                jnp.sum(wave_now * corr_image),
                jnp.sum(correction * corr_image),
                jnp.sum(wave_image * corr_image),
                jnp.sum(corr_image * corr_image),
            ),
            "sector",
        )
        off_diag = 0.5 * (cross_one / cells + cross_two / cells)
        corr_energy = corr_sum / cells
        half_gap = 0.5 * (rayleigh - corr_energy)
        rotation = 0.5 * jnp.arctan2(-off_diag, -half_gap)
        energy = 0.5 * (rayleigh + corr_energy) - jnp.sqrt(
            half_gap * half_gap + off_diag * off_diag
        )
        cosine = jnp.cos(rotation)
        sine = jnp.sin(rotation)
        wave_now = cosine * wave_now + sine * correction
        wave_image = cosine * wave_image + sine * corr_image
    return (wave_now, jnp.reshape(energy, (1,)))


def solution(mesh):
    placed = (
        P("site", "sector", None, None),
        P("site", "sector", None, None, None, None),
        P("sector", None, None, None, None),
        P("site", "sector", None, None, None, None),
        P("site", "sector", None),
        P("site", "sector"),
    )
    return jax.shard_map(
        per_device,
        mesh=mesh,
        in_specs=placed,
        out_specs=(P("site", "sector", None, None), P("site")),
        check_vma=False,
    )
```

profile of v0, /device:TPU:128, one launch (start us, length us, event | category | flops | bytes accessed | tf_op | source)
XLA Modules:
  0.0 1829.7 jit_solution(1440629177672707505)
XLA Ops:
  0.6 1.5 multiply_reduce_fusion.8
  2.1 2.9 collective-permute-start
  5.0 67.7 %psum.287 = f32[]{:T(128)} all-reduce(f32[]{:T(128)} %multiply_reduce_fusion.8), channel_id=1, replica_groups=mesh['site'=8,'sector'=32] {'sector'}, use_global_device_ids=true, to_apply=%region_1.2 | all-reduce | flops 1 | bytes 8 | tf_op jit(solution)/shard_map/psum | solution.py:57
  75.5 1.3 collective-permute-start.2
  78.1 1.3 collective-permute-start.4
  80.2 5.4 collective-permute-done.4
  86.3 2.2 bitcast_select_fusion
  88.7 4.1 while.90
  93.5 64.6 %psum.288 = f32[]{:T(128)} all-reduce(f32[]{:T(128)} %fusion.165), channel_id=1, replica_groups=mesh['site'=8,'sector'=32] {'sector'}, use_global_device_ids=true, to_apply=%region_5.7 | all-reduce | flops 1 | bytes 8 | tf_op jit(solution)/shard_map/psum | solution.py:63
  159.4 63.3 %psum.289 = f32[]{:T(128)} all-reduce(f32[]{:T(128)} %multiply_reduce_fusion.7), channel_id=1, replica_groups=mesh['site'=8,'sector'=32] {'sector'}, use_global_device_ids=true, to_apply=%region_7.9 | all-reduce | flops 1 | bytes 8 | tf_op jit(solution)/shard_map/psum | solution.py:65
  224.0 1.8 collective-permute-start.5
  231.5 4.4 collective-permute-done.8
  236.4 1.5 gather_fusion.1
  238.0 4.1 while.91
  244.2 65.0 %all-reduce.7 = (f32[]{:T(128)}, f32[]{:T(128)}) all-reduce(f32[]{:T(128)S(6)} %div.168, f32[]{:T(128)} %get-tuple-element.330), channel_id=1, replica_groups=mesh['site'=8,'sector'=32] {'sector'}, use_global_device_ids=true, to_apply=%region_9.11 | all-reduce | flops 2 | bytes 16 | tf_op jit(solution)/shard_map/psum | solution.py:68
  311.4 63.3 %psum.293 = f32[]{:T(128)} all-reduce(f32[]{:T(128)} %get-tuple-element.489), channel_id=1, replica_groups=mesh['site'=8,'sector'=32] {'sector'}, use_global_device_ids=true, to_apply=%region_17.19 | all-reduce | flops 1 | bytes 8 | tf_op jit(solution)/shard_map/psum | solution.py:63
  376.0 63.3 %psum.294 = f32[]{:T(128)} all-reduce(f32[]{:T(128)} %multiply_reduce_fusion.6), channel_id=1, replica_groups=mesh['site'=8,'sector'=32] {'sector'}, use_global_device_ids=true, to_apply=%region_19.21 | all-reduce | flops 1 | bytes 8 | tf_op jit(solution)/shard_map/psum | solution.py:65
  440.6 1.8 collective-permute-start.9
  444.9 1.3 collective-permute-start.12
  448.1 4.4 collective-permute-done.12
  453.0 1.5 gather_fusion.2
  454.6 4.1 while.92
  460.8 65.0 %all-reduce.6 = (f32[]{:T(128)}, f32[]{:T(128)}) all-reduce(f32[]{:T(128)S(6)} %div.174, f32[]{:T(128)} %get-tuple-element.327), channel_id=1, replica_groups=mesh['site'=8,'sector'=32] {'sector'}, use_global_device_ids=true, to_apply=%region_21.23 | all-reduce | flops 2 | bytes 16 | tf_op jit(solution)/shard_map/psum | solution.py:68
  528.0 63.3 %psum.298 = f32[]{:T(128)} all-reduce(f32[]{:T(128)} %get-tuple-element.484), channel_id=1, replica_groups=mesh['site'=8,'sector'=32] {'sector'}, use_global_device_ids=true, to_apply=%region_29.31 | all-reduce | flops 1 | bytes 8 | tf_op jit(solution)/shard_map/psum | solution.py:63
  592.5 63.3 %psum.299 = f32[]{:T(128)} all-reduce(f32[]{:T(128)} %multiply_reduce_fusion.5), channel_id=1, replica_groups=mesh['site'=8,'sector'=32] {'sector'}, use_global_device_ids=true, to_apply=%region_31.33 | all-reduce | flops 1 | bytes 8 | tf_op jit(solution)/shard_map/psum | solution.py:65
  657.1 1.8 collective-permute-start.13
  664.6 4.4 collective-permute-done.16
  669.6 1.5 gather_fusion.3
  671.2 4.1 while.93
  677.4 65.0 %all-reduce.5 = (f32[]{:T(128)}, f32[]{:T(128)}) all-reduce(f32[]{:T(128)S(6)} %div.180, f32[]{:T(128)} %get-tuple-element.324), channel_id=1, replica_groups=mesh['site'=8,'sector'=32] {'sector'}, use_global_device_ids=true, to_apply=%region_33.35 | all-reduce | flops 2 | bytes 16 | tf_op jit(solution)/shard_map/psum | solution.py:68
  744.5 63.3 %psum.303 = f32[]{:T(128)} all-reduce(f32[]{:T(128)} %get-tuple-element.479), channel_id=1, replica_groups=mesh['site'=8,'sector'=32] {'sector'}, use_global_device_ids=true, to_apply=%region_41.43 | all-reduce | flops 1 | bytes 8 | tf_op jit(solution)/shard_map/psum | solution.py:63
  809.1 63.3 %psum.304 = f32[]{:T(128)} all-reduce(f32[]{:T(128)} %multiply_reduce_fusion.4), channel_id=1, replica_groups=mesh['site'=8,'sector'=32] {'sector'}, use_global_device_ids=true, to_apply=%region_43.45 | all-reduce | flops 1 | bytes 8 | tf_op jit(solution)/shard_map/psum | solution.py:65
  873.7 1.8 collective-permute-start.17
  881.2 4.4 collective-permute-done.20
  886.2 1.5 gather_fusion.4
  887.8 4.1 while.94
  893.9 65.0 %all-reduce.4 = (f32[]{:T(128)}, f32[]{:T(128)}) all-reduce(f32[]{:T(128)S(6)} %div.186, f32[]{:T(128)} %get-tuple-element.321), channel_id=1, replica_groups=mesh['site'=8,'sector'=32] {'sector'}, use_global_device_ids=true, to_apply=%region_45.47 | all-reduce | flops 2 | bytes 16 | tf_op jit(solution)/shard_map/psum | solution.py:68
  961.1 63.3 %psum.308 = f32[]{:T(128)} all-reduce(f32[]{:T(128)} %get-tuple-element.474), channel_id=1, replica_groups=mesh['site'=8,'sector'=32] {'sector'}, use_global_device_ids=true, to_apply=%region_53.55 | all-reduce | flops 1 | bytes 8 | tf_op jit(solution)/shard_map/psum | solution.py:63
  1025.7 63.3 %psum.309 = f32[]{:T(128)} all-reduce(f32[]{:T(128)} %multiply_reduce_fusion.3), channel_id=1, replica_groups=mesh['site'=8,'sector'=32] {'sector'}, use_global_device_ids=true, to_apply=%region_55.57 | all-reduce | flops 1 | bytes 8 | tf_op jit(solution)/shard_map/psum | solution.py:65
  1090.3 1.8 collective-permute-start.21
  1097.8 4.4 collective-permute-done.24
  1102.7 1.5 gather_fusion.5
  1104.3 4.1 while.95
  1110.5 65.0 %all-reduce.3 = (f32[]{:T(128)}, f32[]{:T(128)}) all-reduce(f32[]{:T(128)S(6)} %div.192, f32[]{:T(128)} %get-tuple-element.318), channel_id=1, replica_groups=mesh['site'=8,'sector'=32] {'sector'}, use_global_device_ids=true, to_apply=%region_57.59 | all-reduce | flops 2 | bytes 16 | tf_op jit(solution)/shard_map/psum | solution.py:68
  1177.7 63.3 %psum.313 = f32[]{:T(128)} all-reduce(f32[]{:T(128)} %get-tuple-element.469), channel_id=1, replica_groups=mesh['site'=8,'sector'=32] {'sector'}, use_global_device_ids=true, to_apply=%region_65.67 | all-reduce | flops 1 | bytes 8 | tf_op jit(solution)/shard_map/psum | solution.py:63
  1242.2 63.3 %psum.314 = f32[]{:T(128)} all-reduce(f32[]{:T(128)} %multiply_reduce_fusion.2), channel_id=1, replica_groups=mesh['site'=8,'sector'=32] {'sector'}, use_global_device_ids=true, to_apply=%region_67.69 | all-reduce | flops 1 | bytes 8 | tf_op jit(solution)/shard_map/psum | solution.py:65
  1306.8 1.8 collective-permute-start.25
  1314.3 4.4 collective-permute-done.28
  1319.3 1.5 gather_fusion.6
  1320.9 4.1 while.96
  1327.1 65.0 %all-reduce.2 = (f32[]{:T(128)}, f32[]{:T(128)}) all-reduce(f32[]{:T(128)S(6)} %div.198, f32[]{:T(128)} %get-tuple-element.315), channel_id=1, replica_groups=mesh['site'=8,'sector'=32] {'sector'}, use_global_device_ids=true, to_apply=%region_69.71 | all-reduce | flops 2 | bytes 16 | tf_op jit(solution)/shard_map/psum | solution.py:68
  1394.3 63.3 %psum.318 = f32[]{:T(128)} all-reduce(f32[]{:T(128)} %get-tuple-element.464), channel_id=1, replica_groups=mesh['site'=8,'sector'=32] {'sector'}, use_global_device_ids=true, to_apply=%region_77.79 | all-reduce | flops 1 | bytes 8 | tf_op jit(solution)/shard_map/psum | solution.py:63
  1458.8 63.3 %psum.319 = f32[]{:T(128)} all-reduce(f32[]{:T(128)} %multiply_reduce_fusion.1), channel_id=1, replica_groups=mesh['site'=8,'sector'=32] {'sector'}, use_global_device_ids=true, to_apply=%region_79.81 | all-reduce | flops 1 | bytes 8 | tf_op jit(solution)/shard_map/psum | solution.py:65
  1523.4 1.8 collective-permute-start.29
  1530.9 4.4 collective-permute-done.32
  1535.9 1.5 gather_fusion.7
  1537.5 4.1 while.97
  1543.6 65.0 %all-reduce.1 = (f32[]{:T(128)}, f32[]{:T(128)}) all-reduce(f32[]{:T(128)S(6)} %div.204, f32[]{:T(128)} %get-tuple-element.312), channel_id=1, replica_groups=mesh['site'=8,'sector'=32] {'sector'}, use_global_device_ids=true, to_apply=%region_81.83 | all-reduce | flops 2 | bytes 16 | tf_op jit(solution)/shard_map/psum | solution.py:68
  1610.8 63.3 %psum.323 = f32[]{:T(128)} all-reduce(f32[]{:T(128)} %get-tuple-element.459), channel_id=1, replica_groups=mesh['site'=8,'sector'=32] {'sector'}, use_global_device_ids=true, to_apply=%region_89.91 | all-reduce | flops 1 | bytes 8 | tf_op jit(solution)/shard_map/psum | solution.py:63
  1675.4 63.3 %psum.324 = f32[]{:T(128)} all-reduce(f32[]{:T(128)} %multiply_reduce_fusion), channel_id=1, replica_groups=mesh['site'=8,'sector'=32] {'sector'}, use_global_device_ids=true, to_apply=%region_91.93 | all-reduce | flops 1 | bytes 8 | tf_op jit(solution)/shard_map/psum | solution.py:65
  1740.0 1.8 collective-permute-start.33
  1746.3 5.8 collective-permute-done.36
  1754.3 4.1 while.98
  1760.5 64.6 %all-reduce = (f32[]{:T(128)}, f32[]{:T(128)}) all-reduce(f32[]{:T(128)S(6)} %div.210, f32[]{:T(128)} %get-tuple-element.309), channel_id=1, replica_groups=mesh['site'=8,'sector'=32] {'sector'}, use_global_device_ids=true, to_apply=%region_93.95 | all-reduce | flops 2 | bytes 16 | tf_op jit(solution)/shard_map/psum | solution.py:68
  (176 shorter events, 89.3 us)
Async XLA Ops:
  2.1 84.2 %collective-permute-start = (bf16[1,1,4,12,128,128]{5,4,3,2,1,0:T(8,128)(2,1)}, bf16[1,1,4,12,128,128]{5,4,3,2,1,0:T(8,128)(2,1)}, u32[]{:S(2)}, u32[]{:S(2)}) collective-permute-start(bf16[1,1,4,12,128,128]{5,4,3,2,1,0:T(8,128)(2,1)} %param.27), channel_id=1, source_target_pairs={{0,32},{32,64},{64,96},{96,128},{128,160},{160,192},{192,224},{1,3... | collective-permute-start | bytes 4718600 | tf_op jit(solution)/shard_map/ppermute | solution.py:13
  74.2 5.9 collective-permute-start.1
  75.5 4.6 collective-permute-start.2
  76.8 3.3 collective-permute-start.3
  78.1 7.5 collective-permute-start.4
  86.3 2.4 copy-start
  88.7 4.1 copy-start.1
  224.0 5.7 collective-permute-start.5
  225.7 4.5 collective-permute-start.6
  227.0 3.8 collective-permute-start.7
  228.3 7.5 collective-permute-start.8
  440.6 5.7 collective-permute-start.9
  442.3 4.5 collective-permute-start.10
  443.6 3.8 collective-permute-start.11
  444.9 7.5 collective-permute-start.12
  657.1 5.7 collective-permute-start.13
  658.9 4.5 collective-permute-start.14
  660.2 3.8 collective-permute-start.15
  661.5 7.5 collective-permute-start.16
  873.7 5.7 collective-permute-start.17
  875.5 4.5 collective-permute-start.18
  876.8 3.8 collective-permute-start.19
  878.1 7.5 collective-permute-start.20
  1090.3 5.7 collective-permute-start.21
  1092.0 4.5 collective-permute-start.22
  1093.3 3.8 collective-permute-start.23
  1094.6 7.5 collective-permute-start.24
  1306.8 5.7 collective-permute-start.25
  1308.6 4.5 collective-permute-start.26
  1309.9 3.8 collective-permute-start.27
  1311.2 7.5 collective-permute-start.28
  1523.4 5.7 collective-permute-start.29
  1525.2 4.5 collective-permute-start.30
  1526.5 3.8 collective-permute-start.31
  1527.8 7.5 collective-permute-start.32
  1740.0 5.7 collective-permute-start.33
  1741.8 3.9 collective-permute-start.34
  1743.1 3.2 collective-permute-start.35
  1744.4 7.7 collective-permute-start.36
where the time goes:
time: 1830 us
  blocking collectives  1600 us (87%)
  starting transfers between devices  53.1 us (3%)
  waiting for transfers between devices  42.4 us (2%)
  between operations  38.3 us (2%)
  local copies, waits for them, and re-layouts  29.4 us (2%)
  other arithmetic  28.1 us (2%)
  loops' own time  24 us (1%)
    psum x8, blocking collectives, per_device(): lax.psum((jnp.sum(correction * wave_image), jnp.sum(wave_now * corr_image...  520 us
    psum x8, blocking collectives, per_device(): rayleigh = lax.psum(jnp.sum(wave_now * wave_image), 'sector') / cells  508 us
    psum x8, blocking collectives, per_device(): resid_norm = lax.psum(jnp.sum(residual * residual), 'sector') / cells  506 us
    psum x1, blocking collectives, per_device(): lax.psum(jnp.sum(initial_state * initial_state), 'sector') / cells  67.7 us
    ppermute x37, starting transfers between devices, passed_along(): return lax.ppermute(x, axis, pairs)  53.1 us
    ppermute x37, waiting for transfers between devices, passed_along(): return lax.ppermute(x, axis, pairs)  42.4 us
  transfers between devices with their start and end apart: 37, of which 10 were waited for; matrix products, arithmetic and copies ran while one was open for 1% of the time, Pallas kernels for 0%

commit v1 on v0

v1 whole, which is shorter than its diff:
```python
import functools

import jax
import jax.numpy as jnp
from jax import lax
from jax.experimental import pallas as pl
from jax.experimental.pallas import tpu as pltpu
from jax.sharding import PartitionSpec as P

GRID = 4
ITERS = 8
GROUP = 3
HALO = jnp.bfloat16
EPS = 1e-06
MESH = pl.DeviceIdType.MESH
F32 = jnp.float32
BF16 = jnp.bfloat16


def kernel(
    blocks, cells, sites, nsrc, terms,
    start_ref, left_ref, edge_ref, right_ref, ids_ref, live_ref,
    state_ref, energy_ref,
    env, renv, xs, ys, ts, zown, start_halo, zsend, zhalo_even, zhalo_odd, row_send, rows,
    env_send, env_recv, renv_sem, start_send, start_recv,
    halo_send, halo_recv, row_send_sem, row_recv_sem,
):
    site = lax.axis_index("site")
    me = lax.axis_index("sector")
    width = start_ref.shape[-1]
    steps = [(p, g) for p in range(nsrc // 2) for g in range(terms // GROUP)]

    def peer(by):
        return lax.rem(me + by + blocks, blocks)

    barrier = pltpu.get_barrier_semaphore()

    @pl.when(site > 0)
    def _():
        pl.semaphore_signal(barrier, inc=1, device_id={"site": site - 1}, device_id_type=MESH)

    @pl.when(site < sites - 1)
    def _():
        pl.semaphore_signal(barrier, inc=1, device_id={"site": site + 1}, device_id_type=MESH)

    for d in range(1, blocks):
        pl.semaphore_signal(barrier, inc=1, device_id={"sector": peer(d)}, device_id_type=MESH)

    def span(ref, p, g):
        return ref.at[pl.ds(2 * p, 2), pl.ds(g * GROUP * width, GROUP * width), :]

    for i, (p, g) in enumerate(steps):
        pltpu.make_async_copy(span(right_ref, p, g), span(renv, p, g), renv_sem.at[i]).start()

    @pl.when(site == 0)
    def _():
        for i, (p, g) in enumerate(steps):
            pltpu.make_async_copy(span(edge_ref, p, g), span(env, p, g), env_recv.at[i]).start()

    pl.semaphore_wait(
        barrier, blocks - 1 + jnp.where(site > 0, 1, 0) + jnp.where(site < sites - 1, 1, 0)
    )

    def env_copy(i, p, g):
        return pltpu.make_async_remote_copy(
            src_ref=span(left_ref, p, g), dst_ref=span(env, p, g),
            send_sem=env_send.at[i], recv_sem=env_recv.at[i],
            device_id={"site": site + 1}, device_id_type=MESH,
        )

    @pl.when(site < sites - 1)
    def _():
        for i, (p, g) in enumerate(steps):
            env_copy(i, p, g).start()

    hops = (1, -1, GRID, -GRID)
    zhalo = (zhalo_even, zhalo_odd)

    def start_copy(n):
        return pltpu.make_async_remote_copy(
            src_ref=start_ref, dst_ref=start_halo.at[n],
            send_sem=start_send.at[n], recv_sem=start_recv.at[n],
            device_id={"sector": peer(hops[n])}, device_id_type=MESH,
        )

    def halo_copy(n, slot):
        return pltpu.make_async_remote_copy(
            src_ref=zsend.at[slot], dst_ref=zhalo[slot].at[n],
            send_sem=halo_send.at[slot, n], recv_sem=halo_recv.at[slot, n],
            device_id={"sector": peer(hops[n])}, device_id_type=MESH,
        )

    def send_rows(values, slot):
        lane = lax.broadcasted_iota(jnp.int32, (1, width), 1)
        row = jnp.zeros((1, width), F32)
        for n, value in enumerate(values):
            row = jnp.where(lane == n, value, row)
        row_send[slot] = row
        rows[slot, me] = row
        for d in range(1, blocks):
            pltpu.make_async_remote_copy(
                src_ref=row_send.at[slot], dst_ref=rows.at[slot, me],
                send_sem=row_send_sem.at[slot], recv_sem=row_recv_sem.at[slot],
                device_id={"sector": peer(d)}, device_id_type=MESH,
            ).start()

    def wait_rows(slot, count):
        pltpu.make_async_copy(
            rows.at[slot, pl.ds(0, blocks - 1)], rows.at[slot, pl.ds(0, blocks - 1)], row_recv_sem.at[slot]
        ).wait()
        total = jnp.sum(rows[slot], axis=0)
        return [total[:, n:n + 1] / cells for n in range(count)]

    def wait_rows_sent(slot):
        pltpu.make_async_copy(
            rows.at[slot, pl.ds(0, blocks - 1)], rows.at[slot, pl.ds(0, blocks - 1)], row_send_sem.at[slot]
        ).wait()

    def inner(a, b):
        return jnp.sum(jnp.sum(a * b, axis=0, keepdims=True), axis=1, keepdims=True)

    places = []
    for j in range(1, nsrc):
        offset = ids_ref[j] - me
        places.append(jnp.where(offset == -1, 0, jnp.where(offset == 1, 1, jnp.where(offset == -GRID, 2, 3))))
    alive = [(j < live_ref[0]).astype(F32) for j in range(nsrc)]

    def multiply(pieces, wait):
        total = jnp.zeros((width, width), F32)
        blank = jnp.zeros((width, width), BF16)
        for i, (p, g) in enumerate(steps):
            if wait:
                pltpu.make_async_copy(span(renv, p, g), span(renv, p, g), renv_sem.at[i]).wait()
                pltpu.make_async_copy(span(env, p, g), span(env, p, g), env_recv.at[i]).wait()
            weights = jnp.concatenate([
                jnp.concatenate([pieces[2 * p], blank], axis=1),
                jnp.concatenate([blank, pieces[2 * p + 1]], axis=1),
            ], axis=0)
            at = slice(g * GROUP * width, (g + 1) * GROUP * width)
            both = jnp.concatenate([env[2 * p, at, :], env[2 * p + 1, at, :]], axis=1)
            product = jnp.dot(both, weights, preferred_element_type=F32).astype(BF16)
            lhs = jnp.concatenate([product[w * width:(w + 1) * width] for w in range(GROUP)], axis=1)
            rhs = []
            for w in range(GROUP):
                at = slice((g * GROUP + w) * width, (g * GROUP + w + 1) * width)
                rhs += [renv[2 * p, at, :], renv[2 * p + 1, at, :]]
            total = total + jnp.dot(lhs, jnp.concatenate(rhs, axis=0), preferred_element_type=F32)
        return total

    for n in range(4):
        start_copy(n).start()
    start = start_ref[...]
    send_rows([inner(start, start)], 1)
    for n in range(4):
        start_copy(n).wait()
    (norm,) = wait_rows(1, 1)
    wait_rows_sent(1)
    scale = lax.rsqrt(norm + EPS)
    xx_start = norm / (norm + EPS)
    pieces = []
    for j in range(nsrc):
        block = (start if j == 0 else start_halo[places[j - 1]]) * scale
        ts[j] = block
        xs[j] = jnp.zeros((width, width), F32)
        ys[j] = jnp.zeros((width, width), F32)
        pieces.append((block * alive[j]).astype(BF16))

    def share(z, slot, halo):
        zown[...] = z
        if halo:
            zsend[slot] = z.astype(HALO)
            for n in range(4):
                halo_copy(n, slot).start()
        send_rows([inner(xs[0], z), inner(ts[0], z), inner(ys[0], z), inner(z, z)], slot)

    def rotate(slot, first, a, xx, yy, tt, inv):
        xz, tz, yz, zz = wait_rows(slot, 4)
        off = 0.5 * ((yy - a * a) * inv + xz)
        gap = 0.5 * (a - tz)
        size = jnp.sqrt(gap * gap + off * off)
        energy = 0.5 * (a + tz) - size
        safe = jnp.where(size > 0, size, 1.0)
        major = jnp.sqrt(0.5 + 0.5 * jnp.abs(gap) / safe)
        minor = jnp.abs(off) / safe / (2.0 * major)
        cosine = jnp.where(gap <= 0, major, minor)
        sine = jnp.where(gap <= 0, minor, major) * jnp.where(off >= 0, -1.0, 1.0)
        cosine = jnp.where(first, 0.0, cosine)
        sine = jnp.where(first, 1.0, sine)
        cc, cs, ss = cosine * cosine, cosine * sine, sine * sine
        xt = a * (1.0 - xx) * inv
        new_a = cc * a + 2.0 * cs * off + ss * tz
        new_yy = cc * yy + 2.0 * cs * yz + ss * zz
        new_xx = cc * xx + 2.0 * cs * xt + ss * tt
        rho = jnp.maximum(new_yy - 2.0 * new_a * new_a + new_a * new_a * new_xx, 0.0)
        new_inv = lax.rsqrt(rho + EPS)
        return energy, cosine, sine, new_a, new_xx, new_yy, rho / (rho + EPS), new_inv

    share(multiply(pieces, True), 0, True)

    def round_of(slot, first, carry):
        a, xx, yy, tt, inv = carry
        _, cosine, sine, a, xx, yy, tt, inv = rotate(slot, first, a, xx, yy, tt, inv)
        for n in range(4):
            halo_copy(n, slot).wait()
        wait_rows_sent(slot)
        pieces = []
        for j in range(nsrc):
            z = zown[...] if j == 0 else zhalo[slot][places[j - 1]].astype(F32)
            x = cosine * xs[j] + sine * ts[j]
            y = cosine * ys[j] + sine * z
            t = (y - a * x) * inv
            xs[j] = x
            ys[j] = y
            ts[j] = t
            pieces.append((t * alive[j]).astype(BF16))
        z = multiply(pieces, False)
        share(z, 1 - slot, True)
        return a, xx, yy, tt, inv

    zero = jnp.zeros((1, 1), F32)
    carry = lax.fori_loop(
        0, ITERS // 2,
        lambda k, carry: round_of(1, False, round_of(0, k == 0, carry)),
        (zero, zero, zero, xx_start, zero + 1.0),
    )
    slot = ITERS % 2
    energy, cosine, sine, *_ = rotate(slot, False, *carry)
    state_ref[...] = cosine * xs[0] + sine * ts[0]
    energy_ref[0] = energy[0, 0]
    for n in range(4):
        halo_copy(n, slot).wait()
    wait_rows_sent(slot)

    @pl.when(site < sites - 1)
    def _():
        for i, (p, g) in enumerate(steps):
            env_copy(i, p, g).wait_send()


def per_device(initial_state, left_env, edge_env, right_env, source_blocks, live_terms):
    nsrc, terms, width = left_env.shape[2], left_env.shape[3], left_env.shape[4]
    blocks, sites = lax.axis_size("sector"), lax.axis_size("site")
    count = (nsrc // 2) * (terms // GROUP)
    flat = (nsrc, terms * width, width)
    vmem = pl.BlockSpec(memory_space=pltpu.VMEM)
    smem = pl.BlockSpec(memory_space=pltpu.SMEM)
    anywhere = pl.BlockSpec(memory_space=pl.ANY)
    dma = pltpu.SemaphoreType.DMA
    body = functools.partial(kernel, blocks, float(blocks * width * width), sites, nsrc, terms)
    state, energy = pl.pallas_call(
        body,
        out_shape=(
            jax.ShapeDtypeStruct((width, width), F32),
            jax.ShapeDtypeStruct((1,), F32),
        ),
        in_specs=[vmem, anywhere, anywhere, anywhere, smem, smem],
        out_specs=(vmem, smem),
        scratch_shapes=[
            pltpu.VMEM(flat, BF16),
            pltpu.VMEM(flat, BF16),
            pltpu.VMEM((nsrc, width, width), F32),
            pltpu.VMEM((nsrc, width, width), F32),
            pltpu.VMEM((nsrc, width, width), F32),
            pltpu.VMEM((width, width), F32),
            pltpu.VMEM((4, width, width), F32),
            pltpu.VMEM((2, width, width), HALO),
            pltpu.VMEM((4, width, width), HALO),
            pltpu.VMEM((4, width, width), HALO),
            pltpu.VMEM((2, 1, width), F32),
            pltpu.VMEM((2, blocks, 1, width), F32),
            dma((count,)), dma((count,)), dma((count,)), dma((4,)), dma((4,)),
            dma((2, 4)), dma((2, 4)), dma((2,)), dma((2,)),
        ],
        compiler_params=pltpu.CompilerParams(
            collective_id=0, has_side_effects=True, vmem_limit_bytes=32 * 1024 * 1024
        ),
        name="window",
    )(
        initial_state[0, 0],
        left_env.reshape(flat),
        edge_env.reshape(flat),
        right_env.reshape(flat),
        source_blocks.reshape(nsrc),
        live_terms.reshape(1),
    )
    return state[None, None], energy


def solution(mesh):
    placed = (
        P("site", "sector", None, None),
        P("site", "sector", None, None, None, None),
        P("sector", None, None, None, None),
        P("site", "sector", None, None, None, None),
        P("site", "sector", None),
        P("site", "sector"),
    )
    return jax.shard_map(
        per_device,
        mesh=mesh,
        in_specs=placed,
        out_specs=(P("site", "sector", None, None), P("site")),
        check_vma=False,
    )
```

time: 1830 us -> 110 us (0.06)
  blocking collectives: 1600 us -> 0 us
  Pallas kernels: 0 us -> 99 us
  starting transfers between devices: 53.1 us -> 0 us
  waiting for transfers between devices: 42.4 us -> 0 us
  between operations: 38.3 us -> 2.99 us
  other arithmetic: 28.1 us -> 0 us
  loops' own time: 24 us -> 0 us
  local copies, waits for them, and re-layouts: 29.4 us -> 6.34 us
    psum x25 -> x0, blocking collectives: 1600 us -> none  [the longest x8 520 us: per_device(): lax.psum((jnp.sum(correction * wave_image), jnp.sum(wave_now * corr_image...]
    pallas_call x0 -> x1, Pallas kernels: none -> 99 us  [per_device(): pl.pallas_call(body, out_shape=(jax.ShapeDtypeStruct((width, width), F32)...]
    ppermute x37 -> x0, starting transfers between devices: 53.1 us -> none  [passed_along(): return lax.ppermute(x, axis, pairs)]
    ppermute x37 -> x0, waiting for transfers between devices: 42.4 us -> none  [passed_along(): return lax.ppermute(x, axis, pairs)]
    another operation x9 -> x0, loops' own time: 24 us -> none  [operate(): lax.fori_loop(0, live_count, add_term, jnp.zeros((width, width), jnp.floa...]
  transfers between devices with their start and end apart: 37 -> 0, of which waited for: 10 -> 0; matrix products, arithmetic and copies ran while one was open for 1% -> 0% of each run, Pallas kernels for 0% -> 0%
where the time goes in v1:
time: 110 us; the launch traced here: 108 us
  Pallas kernels  99 us (90%)
  local copies, waits for them, and re-layouts  6.34 us (6%)
  between operations  2.99 us (3%)
    pallas_call x1, Pallas kernels, per_device(): pl.pallas_call(body, out_shape=(jax.ShapeDtypeStruct((width, width), F32)...  99 us
    unnamed x11, local copies, waits for them, and re-layouts  6.34 us

profile of v1, /device:TPU:128, one launch (start us, length us, event | category | flops | bytes accessed | tf_op | source)
XLA Modules:
  0.0 108.4 jit_solution(8427800800670352653)
XLA Ops:
  1.3 0.0 copy-start
  1.3 1.4 %copy-done = bf16[1,1,4,12,128,128]{5,4,3,2,1,0:T(8,128)(2,1)S(1)} copy-done((bf16[1,1,4,12,128,128]{5,4,3,2,1,0:T(8,128)(2,1)S(1)}, bf16[1,1,4,12,128,128]{5,4,3,2,1,0:T(8,128)(2,1)}, u32[]{:S(2)}) %copy-start) | copy-done | bytes 1572888
  2.7 0.0 copy-start.1
  2.7 1.4 %copy-done.1 = bf16[1,4,12,128,128]{4,3,2,1,0:T(8,128)(2,1)S(1)} copy-done((bf16[1,4,12,128,128]{4,3,2,1,0:T(8,128)(2,1)S(1)}, bf16[1,4,12,128,128]{4,3,2,1,0:T(8,128)(2,1)}, u32[]{:S(2)}) %copy-start.1) | copy-done | bytes 1572888
  4.1 0.0 copy-start.2
  4.1 1.4 %copy-done.2 = bf16[1,1,4,12,128,128]{5,4,3,2,1,0:T(8,128)(2,1)S(1)} copy-done((bf16[1,1,4,12,128,128]{5,4,3,2,1,0:T(8,128)(2,1)S(1)}, bf16[1,1,4,12,128,128]{5,4,3,2,1,0:T(8,128)(2,1)}, u32[]{:S(2)}) %copy-start.2) | copy-done | bytes 1572888
  5.5 0.0 copy-start.3
  5.5 0.8 copy-done.3
  6.3 0.0 copy-start.4
  6.3 0.7 copy-done.4
  7.0 99.0 %window.1 = (f32[128,128]{1,0:T(8,128)S(1)}, f32[1]{0:T(128)}) custom-call(f32[128,128]{1,0:T(8,128)S(1)} %bitcast.12, bf16[4,1536,128]{2,1,0:T(8,128)(2,1)S(1)} %bitcast.8, bf16[4,1536,128]{2,1,0:T(8,128)(2,1)S(1)} %bitcast.9, bf16[4,1536,128]{2,1,0:T(8,128)(2,1)S(1)} %bitcast.10, s32[4]{0:T(128)S(1)} %bitcast.13, s32[1]{0:T(128)} %bitcast.7.live_ref), custom_call_target="tpu_custom_call" | custom-call | tf_op jit(solution)/shard_map/window/pallas_call | solution.py:250
  106.0 0.6 copy.11
Async XLA Ops:
  1.3 1.4 %copy-start = (bf16[1,1,4,12,128,128]{5,4,3,2,1,0:T(8,128)(2,1)S(1)}, bf16[1,1,4,12,128,128]{5,4,3,2,1,0:T(8,128)(2,1)}, u32[]{:S(2)}) copy-start(bf16[1,1,4,12,128,128]{5,4,3,2,1,0:T(8,128)(2,1)} %param.7) | copy-start | bytes 4718596
  2.7 1.4 %copy-start.1 = (bf16[1,4,12,128,128]{4,3,2,1,0:T(8,128)(2,1)S(1)}, bf16[1,4,12,128,128]{4,3,2,1,0:T(8,128)(2,1)}, u32[]{:S(2)}) copy-start(bf16[1,4,12,128,128]{4,3,2,1,0:T(8,128)(2,1)} %param.8) | copy-start | bytes 4718596
  4.1 1.4 %copy-start.2 = (bf16[1,1,4,12,128,128]{5,4,3,2,1,0:T(8,128)(2,1)S(1)}, bf16[1,1,4,12,128,128]{5,4,3,2,1,0:T(8,128)(2,1)}, u32[]{:S(2)}) copy-start(bf16[1,1,4,12,128,128]{5,4,3,2,1,0:T(8,128)(2,1)} %param.9) | copy-start | bytes 4718596
  5.5 0.8 copy-start.3
  6.3 0.7 copy-start.4

commit v2 on v1

--- a/solution.py
+++ b/solution.py
@@ -10,7 +10,9 @@
 GRID = 4
 ITERS = 8
 GROUP = 3
+LATE_FIRST = 3
 HALO = jnp.bfloat16
+PART = jnp.bfloat16
 EPS = 1e-06
 MESH = pl.DeviceIdType.MESH
 F32 = jnp.float32
@@ -21,14 +23,20 @@
     blocks, cells, sites, nsrc, terms,
     start_ref, left_ref, edge_ref, right_ref, ids_ref, live_ref,
     state_ref, energy_ref,
-    env, renv, xs, ys, ts, zown, start_halo, zsend, zhalo_even, zhalo_odd, row_send, rows,
-    env_send, env_recv, renv_sem, start_send, start_recv,
+    env, renv, help_env, help_renv, xs, ys, ts, zown, start_halo, zsend, zhalo_even, zhalo_odd, row_send, rows,
+    piece_send, piece_in, part_send, part_in,
+    env_send, env_recv, renv_sem, start_sem, start_send, start_recv,
     halo_send, halo_recv, row_send_sem, row_recv_sem,
+    help_env_sem, help_renv_send, help_renv_recv, piece_sends, piece_recvs, part_sends, part_recvs,
 ):
     site = lax.axis_index("site")
     me = lax.axis_index("sector")
     width = start_ref.shape[-1]
-    steps = [(p, g) for p in range(nsrc // 2) for g in range(terms // GROUP)]
+    groups = terms // GROUP
+    steps = [(p, g) for p in range(nsrc // 2) for g in range(groups)]
+    early = [i for i, (p, _) in enumerate(steps) if p == 0]
+    late = [i for i, (p, _) in enumerate(steps) if p == 1]
+    first_site, last_site = site == 0, site == sites - 1
 
     def peer(by):
         return lax.rem(me + by + blocks, blocks)
@@ -49,29 +57,61 @@
     def span(ref, p, g):
         return ref.at[pl.ds(2 * p, 2), pl.ds(g * GROUP * width, GROUP * width), :]
 
+    pltpu.make_async_copy(start_ref, zown, start_sem).start()
     for i, (p, g) in enumerate(steps):
         pltpu.make_async_copy(span(right_ref, p, g), span(renv, p, g), renv_sem.at[i]).start()
 
-    @pl.when(site == 0)
+    @pl.when(first_site)
     def _():
         for i, (p, g) in enumerate(steps):
             pltpu.make_async_copy(span(edge_ref, p, g), span(env, p, g), env_recv.at[i]).start()
+
+    @pl.when(jnp.logical_not(last_site))
+    def _():
+        pltpu.make_async_copy(left_ref.at[pl.ds(2, 2)], help_env, help_env_sem).start()
 
     pl.semaphore_wait(
         barrier, blocks - 1 + jnp.where(site > 0, 1, 0) + jnp.where(site < sites - 1, 1, 0)
     )
 
-    def env_copy(i, p, g):
+    def env_copy(i):
+        p, g = steps[i]
         return pltpu.make_async_remote_copy(
             src_ref=span(left_ref, p, g), dst_ref=span(env, p, g),
             send_sem=env_send.at[i], recv_sem=env_recv.at[i],
             device_id={"site": site + 1}, device_id_type=MESH,
         )
 
-    @pl.when(site < sites - 1)
-    def _():
-        for i, (p, g) in enumerate(steps):
-            env_copy(i, p, g).start()
+    def help_copy(g):
+        return pltpu.make_async_remote_copy(
+            src_ref=span(right_ref, 1, g), dst_ref=span(help_renv, 0, g),
+            send_sem=help_renv_send.at[g], recv_sem=help_renv_recv.at[g],
+            device_id={"site": site - 1}, device_id_type=MESH,
+        )
+
+    def piece_copy(n):
+        return pltpu.make_async_remote_copy(
+            src_ref=piece_send.at[n], dst_ref=piece_in.at[n],
+            send_sem=piece_sends.at[n], recv_sem=piece_recvs.at[n],
+            device_id={"site": site - 1}, device_id_type=MESH,
+        )
+
+    def part_copy(n):
+        return pltpu.make_async_remote_copy(
+            src_ref=part_send.at[n], dst_ref=part_in.at[n],
+            send_sem=part_sends.at[n], recv_sem=part_recvs.at[n],
+            device_id={"site": site + 1}, device_id_type=MESH,
+        )
+
+    @pl.when(jnp.logical_not(last_site))
+    def _():
+        for i in early:
+            env_copy(i).start()
+
+    @pl.when(jnp.logical_not(first_site))
+    def _():
+        for g in range(groups - 1):
+            help_copy(g).start()
 
     hops = (1, -1, GRID, -GRID)
     zhalo = (zhalo_even, zhalo_odd)
@@ -125,31 +165,94 @@
         places.append(jnp.where(offset == -1, 0, jnp.where(offset == 1, 1, jnp.where(offset == -GRID, 2, 3))))
     alive = [(j < live_ref[0]).astype(F32) for j in range(nsrc)]
 
-    def multiply(pieces, wait):
-        total = jnp.zeros((width, width), F32)
+    def multiply(total, e_ref, r_ref, p, two, wait=None):
+        size = GROUP if wait else terms
         blank = jnp.zeros((width, width), BF16)
-        for i, (p, g) in enumerate(steps):
+        weights = jnp.concatenate([
+            jnp.concatenate([two[0], blank], axis=1),
+            jnp.concatenate([blank, two[1]], axis=1),
+        ], axis=0)
+        for g in range(terms // size):
             if wait:
-                pltpu.make_async_copy(span(renv, p, g), span(renv, p, g), renv_sem.at[i]).wait()
-                pltpu.make_async_copy(span(env, p, g), span(env, p, g), env_recv.at[i]).wait()
-            weights = jnp.concatenate([
-                jnp.concatenate([pieces[2 * p], blank], axis=1),
-                jnp.concatenate([blank, pieces[2 * p + 1]], axis=1),
-            ], axis=0)
-            at = slice(g * GROUP * width, (g + 1) * GROUP * width)
-            both = jnp.concatenate([env[2 * p, at, :], env[2 * p + 1, at, :]], axis=1)
+                wait(g)
+            at = slice(g * size * width, (g + 1) * size * width)
+            both = jnp.concatenate([e_ref[2 * p, at, :], e_ref[2 * p + 1, at, :]], axis=1)
             product = jnp.dot(both, weights, preferred_element_type=F32).astype(BF16)
-            lhs = jnp.concatenate([product[w * width:(w + 1) * width] for w in range(GROUP)], axis=1)
+            lhs = jnp.concatenate([product[w * width:(w + 1) * width] for w in range(size)], axis=1)
             rhs = []
-            for w in range(GROUP):
-                at = slice((g * GROUP + w) * width, (g * GROUP + w + 1) * width)
-                rhs += [renv[2 * p, at, :], renv[2 * p + 1, at, :]]
+            for w in range(size):
+                at = slice((g * size + w) * width, (g * size + w + 1) * width)
+                rhs += [r_ref[2 * p, at, :], r_ref[2 * p + 1, at, :]]
             total = total + jnp.dot(lhs, jnp.concatenate(rhs, axis=0), preferred_element_type=F32)
         return total
 
+    def wait_env(i):
+        pltpu.make_async_copy(span(env, *steps[i]), span(env, *steps[i]), env_recv.at[i]).wait()
+
+    nothing = jnp.zeros((width, width), F32)
+
+    def shared_multiply(n, pieces):
+        piece_send[n, 0] = pieces[2]
+        piece_send[n, 1] = pieces[3]
+
+        @pl.when(jnp.logical_not(first_site))
+        def _():
+            piece_copy(n).start()
+            if n == 0:
+                help_copy(groups - 1).start()
+
+        @pl.when(jnp.logical_not(last_site))
+        def _():
+            piece = pltpu.make_async_copy(piece_in.at[n], piece_in.at[n], piece_recvs.at[n])
+            piece.wait()
+            if n == 0:
+                pltpu.make_async_copy(help_env, help_env, help_env_sem).wait()
+
+            def arrived(g):
+                pltpu.make_async_copy(
+                    span(help_renv, 0, g), span(help_renv, 0, g), help_renv_recv.at[g]
+                ).wait()
+
+            part_send[n] = multiply(
+                nothing, help_env, help_renv, 0, [piece_in[n, 0], piece_in[n, 1]], None if n else arrived
+            ).astype(PART)
+            part_copy(n).start()
+            for i in (late[:LATE_FIRST], late[LATE_FIRST:])[n]:
+                env_copy(i).start()
+
+        if n == 0:
+            for i, (p, g) in enumerate(steps):
+                pltpu.make_async_copy(span(renv, p, g), span(renv, p, g), renv_sem.at[i]).wait()
+        total = multiply(
+            nothing, env, renv, 0, pieces[:2], None if n else lambda g: wait_env(early[g])
+        )
+
+        @pl.when(first_site)
+        def _():
+            if n == 0:
+                for i in late:
+                    wait_env(i)
+            part_in[n] = multiply(nothing, env, renv, 1, pieces[2:]).astype(PART)
+
+        @pl.when(jnp.logical_not(first_site))
+        def _():
+            pltpu.make_async_copy(part_in.at[n], part_in.at[n], part_recvs.at[n]).wait()
+
+        return total + part_in[n].astype(F32)
+
+    def local_multiply(pieces, wait):
+        total = multiply(nothing, env, renv, 0, pieces[:2])
+        if wait:
+            @pl.when(jnp.logical_not(first_site))
+            def _():
+                for i in late:
+                    wait_env(i)
+        return multiply(total, env, renv, 1, pieces[2:])
+
     for n in range(4):
         start_copy(n).start()
-    start = start_ref[...]
+    pltpu.make_async_copy(start_ref, zown, start_sem).wait()
+    start = zown[...]
     send_rows([inner(start, start)], 1)
     for n in range(4):
         start_copy(n).wait()
@@ -177,15 +280,17 @@
         xz, tz, yz, zz = wait_rows(slot, 4)
         off = 0.5 * ((yy - a * a) * inv + xz)
         gap = 0.5 * (a - tz)
-        size = jnp.sqrt(gap * gap + off * off)
-        energy = 0.5 * (a + tz) - size
-        safe = jnp.where(size > 0, size, 1.0)
-        major = jnp.sqrt(0.5 + 0.5 * jnp.abs(gap) / safe)
-        minor = jnp.abs(off) / safe / (2.0 * major)
+        square = gap * gap + off * off
+        over = jnp.where(square > 0, lax.rsqrt(jnp.where(square > 0, square, 1.0)), 0.0)
+        energy = 0.5 * (a + tz) - square * over
+        half = 0.5 + 0.5 * jnp.abs(gap) * over
+        turn = lax.rsqrt(half)
+        major = half * turn
+        minor = 0.5 * jnp.abs(off) * over * turn
         cosine = jnp.where(gap <= 0, major, minor)
         sine = jnp.where(gap <= 0, minor, major) * jnp.where(off >= 0, -1.0, 1.0)
-        cosine = jnp.where(first, 0.0, cosine)
-        sine = jnp.where(first, 1.0, sine)
+        if first:
+            cosine, sine = jnp.zeros_like(gap), jnp.ones_like(gap)
         cc, cs, ss = cosine * cosine, cosine * sine, sine * sine
         xt = a * (1.0 - xx) * inv
         new_a = cc * a + 2.0 * cs * off + ss * tz
@@ -195,14 +300,13 @@
         new_inv = lax.rsqrt(rho + EPS)
         return energy, cosine, sine, new_a, new_xx, new_yy, rho / (rho + EPS), new_inv
 
-    share(multiply(pieces, True), 0, True)
-
-    def round_of(slot, first, carry):
+    share(shared_multiply(0, pieces), 0, True)
+
+    def round_of(slot, first, carry, apply):
         a, xx, yy, tt, inv = carry
         _, cosine, sine, a, xx, yy, tt, inv = rotate(slot, first, a, xx, yy, tt, inv)
         for n in range(4):
-            halo_copy(n, slot).wait()
-        wait_rows_sent(slot)
+            halo_copy(n, slot).wait_recv()
         pieces = []
         for j in range(nsrc):
             z = zown[...] if j == 0 else zhalo[slot][places[j - 1]].astype(F32)
@@ -213,16 +317,24 @@
             ys[j] = y
             ts[j] = t
             pieces.append((t * alive[j]).astype(BF16))
-        z = multiply(pieces, False)
+        z = apply(pieces)
+        for n in range(4):
+            halo_copy(n, slot).wait_send()
+        wait_rows_sent(slot)
         share(z, 1 - slot, True)
         return a, xx, yy, tt, inv
 
     zero = jnp.zeros((1, 1), F32)
-    carry = lax.fori_loop(
-        0, ITERS // 2,
-        lambda k, carry: round_of(1, False, round_of(0, k == 0, carry)),
-        (zero, zero, zero, xx_start, zero + 1.0),
-    )
+    carry = (zero, zero, zero, xx_start, zero + 1.0)
+    carry = round_of(0, True, carry, lambda pieces: shared_multiply(1, pieces))
+    carry = round_of(1, False, carry, lambda pieces: local_multiply(pieces, True))
+
+    def two_rounds(_, carry):
+        for slot in range(2):
+            carry = round_of(slot, False, carry, lambda pieces: local_multiply(pieces, False))
+        return carry
+
+    carry = lax.fori_loop(0, ITERS // 2 - 1, two_rounds, carry)
     slot = ITERS % 2
     energy, cosine, sine, *_ = rotate(slot, False, *carry)
     state_ref[...] = cosine * xs[0] + sine * ts[0]
@@ -231,10 +343,19 @@
         halo_copy(n, slot).wait()
     wait_rows_sent(slot)
 
-    @pl.when(site < sites - 1)
-    def _():
-        for i, (p, g) in enumerate(steps):
-            env_copy(i, p, g).wait_send()
+    @pl.when(jnp.logical_not(last_site))
+    def _():
+        for i in range(len(steps)):
+            env_copy(i).wait_send()
+        for n in range(2):
+            part_copy(n).wait_send()
+
+    @pl.when(jnp.logical_not(first_site))
+    def _():
+        for g in range(groups):
+            help_copy(g).wait_send()
+        for n in range(2):
+            piece_copy(n).wait_send()
 
 
 def per_device(initial_state, left_env, edge_env, right_env, source_blocks, live_terms):
@@ -253,11 +374,13 @@
             jax.ShapeDtypeStruct((width, width), F32),
             jax.ShapeDtypeStruct((1,), F32),
         ),
-        in_specs=[vmem, anywhere, anywhere, anywhere, smem, smem],
+        in_specs=[anywhere, anywhere, anywhere, anywhere, smem, smem],
         out_specs=(vmem, smem),
         scratch_shapes=[
             pltpu.VMEM(flat, BF16),
             pltpu.VMEM(flat, BF16),
+            pltpu.VMEM((2, *flat[1:]), BF16),
+            pltpu.VMEM((2, *flat[1:]), BF16),
             pltpu.VMEM((nsrc, width, width), F32),
             pltpu.VMEM((nsrc, width, width), F32),
             pltpu.VMEM((nsrc, width, width), F32),
@@ -268,11 +391,16 @@
             pltpu.VMEM((4, width, width), HALO),
             pltpu.VMEM((2, 1, width), F32),
             pltpu.VMEM((2, blocks, 1, width), F32),
-            dma((count,)), dma((count,)), dma((count,)), dma((4,)), dma((4,)),
+            pltpu.VMEM((2, 2, width, width), BF16),
+            pltpu.VMEM((2, 2, width, width), BF16),
+            pltpu.VMEM((2, width, width), PART),
+            pltpu.VMEM((2, width, width), PART),
+            dma((count,)), dma((count,)), dma((count,)), dma, dma((4,)), dma((4,)),
             dma((2, 4)), dma((2, 4)), dma((2,)), dma((2,)),
+            dma, dma((count // 2,)), dma((count // 2,)), dma((2,)), dma((2,)), dma((2,)), dma((2,)),
         ],
         compiler_params=pltpu.CompilerParams(
-            collective_id=0, has_side_effects=True, vmem_limit_bytes=32 * 1024 * 1024
+            collective_id=0, has_side_effects=True, vmem_limit_bytes=60 * 1024 * 1024
         ),
         name="window",
     )(

time: 110 us -> 102 us (0.927)
  local copies, waits for them, and re-layouts: 6.34 us -> 1.47 us
  Pallas kernels: 99 us -> 96.7 us
    unnamed x11 -> x1, local copies, waits for them, and re-layouts: 6.34 us -> 1.47 us
    pallas_call x1, Pallas kernels: 99 us -> 96.7 us  [per_device(): pl.pallas_call(body, out_shape=(jax.ShapeDtypeStruct((width, width), F32)...]
where the time goes in v2:
time: 102 us; the launch traced here: 101 us
  Pallas kernels  96.7 us (95%)
  between operations  3.03 us (3%)
  local copies, waits for them, and re-layouts  1.47 us (1%)
    pallas_call x1, Pallas kernels, per_device(): pl.pallas_call(body, out_shape=(jax.ShapeDtypeStruct((width, width), F32)...  96.7 us

profile of v2, /device:TPU:128, one launch (start us, length us, event | category | flops | bytes accessed | tf_op | source)
XLA Modules:
  0.0 101.2 jit_solution(7914143296863695801)
XLA Ops:
  1.3 96.7 %window.1 = (f32[128,128]{1,0:T(8,128)}, f32[1]{0:T(128)}) custom-call(f32[128,128]{1,0:T(8,128)} %bitcast.12, bf16[4,1536,128]{2,1,0:T(8,128)(2,1)} %bitcast.8, bf16[4,1536,128]{2,1,0:T(8,128)(2,1)} %bitcast.9, bf16[4,1536,128]{2,1,0:T(8,128)(2,1)} %bitcast.10, s32[4]{0:T(128)} %bitcast.13, s32[1]{0:T(128)} %bitcast.7.live_ref), custom_call_target="tpu_custom_call" | custom-call | tf_op jit(solution)/shard_map/window/pallas_call | solution.py:371
  98.0 1.5 %copy.11 = f32[1,1,128,128]{3,2,1,0:T(8,128)} copy(f32[1,1,128,128]{3,2,1,0:T(8,128)} %bitcast.11) | data formatting | bytes 131072

commit v3 on v2

--- a/solution.py
+++ b/solution.py
@@ -23,10 +23,10 @@
     blocks, cells, sites, nsrc, terms,
     start_ref, left_ref, edge_ref, right_ref, ids_ref, live_ref,
     state_ref, energy_ref,
-    env, renv, help_env, help_renv, xs, ys, ts, zown, start_halo, zsend, zhalo_even, zhalo_odd, row_send, rows,
+    env, renv, help_env, help_renv, xs, ys, us, ts, zs, start_halo, zsend, zhalo_even, zhalo_odd, row_send, rows, norm_send, norms,
     piece_send, piece_in, part_send, part_in,
     env_send, env_recv, renv_sem, start_sem, start_send, start_recv,
-    halo_send, halo_recv, row_send_sem, row_recv_sem,
+    halo_send, halo_recv, row_send_sem, row_recv_sem, norm_send_sem, norm_recv_sem,
     help_env_sem, help_renv_send, help_renv_recv, piece_sends, piece_recvs, part_sends, part_recvs,
 ):
     site = lax.axis_index("site")
@@ -51,13 +51,16 @@
     def _():
         pl.semaphore_signal(barrier, inc=1, device_id={"site": site + 1}, device_id_type=MESH)
 
-    for d in range(1, blocks):
-        pl.semaphore_signal(barrier, inc=1, device_id={"sector": peer(d)}, device_id_type=MESH)
+    side = 2 * GRID
+    base, spot, line = me - lax.rem(me, side), lax.rem(me, side), me // side
+    planes = ([base + lax.rem(spot + d, side) for d in range(1, side)], [peer(d) for d in range(side, blocks, side)])
+    for other in planes[0] + planes[1]:
+        pl.semaphore_signal(barrier, inc=1, device_id={"sector": other}, device_id_type=MESH)
 
     def span(ref, p, g):
         return ref.at[pl.ds(2 * p, 2), pl.ds(g * GROUP * width, GROUP * width), :]
 
-    pltpu.make_async_copy(start_ref, zown, start_sem).start()
+    pltpu.make_async_copy(start_ref, zs, start_sem).start()
     for i, (p, g) in enumerate(steps):
         pltpu.make_async_copy(span(right_ref, p, g), span(renv, p, g), renv_sem.at[i]).start()
 
@@ -71,7 +74,7 @@
         pltpu.make_async_copy(left_ref.at[pl.ds(2, 2)], help_env, help_env_sem).start()
 
     pl.semaphore_wait(
-        barrier, blocks - 1 + jnp.where(site > 0, 1, 0) + jnp.where(site < sites - 1, 1, 0)
+        barrier, len(planes[0]) + len(planes[1]) + jnp.where(site > 0, 1, 0) + jnp.where(site < sites - 1, 1, 0)
     )
 
     def env_copy(i):
@@ -129,6 +132,8 @@
             send_sem=halo_send.at[slot, n], recv_sem=halo_recv.at[slot, n],
             device_id={"sector": peer(hops[n])}, device_id_type=MESH,
         )
+
+    far_first = sorted(range(1, blocks), key=lambda d: abs(d - blocks // 2))
 
     def send_rows(values, slot):
         lane = lax.broadcasted_iota(jnp.int32, (1, width), 1)
@@ -137,7 +142,7 @@
             row = jnp.where(lane == n, value, row)
         row_send[slot] = row
         rows[slot, me] = row
-        for d in range(1, blocks):
+        for d in far_first:
             pltpu.make_async_remote_copy(
                 src_ref=row_send.at[slot], dst_ref=rows.at[slot, me],
                 send_sem=row_send_sem.at[slot], recv_sem=row_recv_sem.at[slot],
@@ -165,25 +170,18 @@
         places.append(jnp.where(offset == -1, 0, jnp.where(offset == 1, 1, jnp.where(offset == -GRID, 2, 3))))
     alive = [(j < live_ref[0]).astype(F32) for j in range(nsrc)]
 
-    def multiply(total, e_ref, r_ref, p, two, wait=None):
+    def multiply(total, e_ref, r_ref, jobs, wait=None):
         size = GROUP if wait else terms
-        blank = jnp.zeros((width, width), BF16)
-        weights = jnp.concatenate([
-            jnp.concatenate([two[0], blank], axis=1),
-            jnp.concatenate([blank, two[1]], axis=1),
-        ], axis=0)
         for g in range(terms // size):
             if wait:
                 wait(g)
             at = slice(g * size * width, (g + 1) * size * width)
-            both = jnp.concatenate([e_ref[2 * p, at, :], e_ref[2 * p + 1, at, :]], axis=1)
-            product = jnp.dot(both, weights, preferred_element_type=F32).astype(BF16)
-            lhs = jnp.concatenate([product[w * width:(w + 1) * width] for w in range(size)], axis=1)
-            rhs = []
-            for w in range(size):
-                at = slice((g * size + w) * width, (g * size + w + 1) * width)
-                rhs += [r_ref[2 * p, at, :], r_ref[2 * p + 1, at, :]]
-            total = total + jnp.dot(lhs, jnp.concatenate(rhs, axis=0), preferred_element_type=F32)
+            products = [
+                jnp.dot(e_ref[j, at, :], piece, preferred_element_type=F32).astype(BF16) for j, piece in jobs
+            ]
+            for product, (j, _) in zip(products, jobs):
+                lhs = jnp.concatenate([product[w * width:(w + 1) * width] for w in range(size)], axis=1)
+                total = total + jnp.dot(lhs, r_ref[j, at, :], preferred_element_type=F32)
         return total
 
     def wait_env(i):
@@ -191,7 +189,7 @@
 
     nothing = jnp.zeros((width, width), F32)
 
-    def shared_multiply(n, pieces):
+    def shared_multiply(n, total, pieces):
         piece_send[n, 0] = pieces[2]
         piece_send[n, 1] = pieces[3]
 
@@ -214,7 +212,7 @@
                 ).wait()
 
             part_send[n] = multiply(
-                nothing, help_env, help_renv, 0, [piece_in[n, 0], piece_in[n, 1]], None if n else arrived
+                nothing, help_env, help_renv, [(0, piece_in[n, 0]), (1, piece_in[n, 1])], None if n else arrived
             ).astype(PART)
             part_copy(n).start()
             for i in (late[:LATE_FIRST], late[LATE_FIRST:])[n]:
@@ -223,16 +221,17 @@
         if n == 0:
             for i, (p, g) in enumerate(steps):
                 pltpu.make_async_copy(span(renv, p, g), span(renv, p, g), renv_sem.at[i]).wait()
-        total = multiply(
-            nothing, env, renv, 0, pieces[:2], None if n else lambda g: wait_env(early[g])
-        )
+        if n == 0:
+            total = multiply(total, env, renv, [(0, pieces[0]), (1, pieces[1])], lambda g: wait_env(early[g]))
+        else:
+            total = multiply(total, env, renv, [(1, pieces[1])])
 
         @pl.when(first_site)
         def _():
             if n == 0:
                 for i in late:
                     wait_env(i)
-            part_in[n] = multiply(nothing, env, renv, 1, pieces[2:]).astype(PART)
+            part_in[n] = multiply(nothing, env, renv, [(2, pieces[2]), (3, pieces[3])]).astype(PART)
 
         @pl.when(jnp.logical_not(first_site))
         def _():
@@ -240,41 +239,58 @@
 
         return total + part_in[n].astype(F32)
 
-    def local_multiply(pieces, wait):
-        total = multiply(nothing, env, renv, 0, pieces[:2])
+    def local_multiply(total, pieces, wait):
         if wait:
             @pl.when(jnp.logical_not(first_site))
             def _():
                 for i in late:
                     wait_env(i)
-        return multiply(total, env, renv, 1, pieces[2:])
-
+        return multiply(total, env, renv, [(j, pieces[j]) for j in range(1, nsrc)])
+
+    pltpu.make_async_copy(start_ref, zs, start_sem).wait()
+    start = zs[...]
+    norm = inner(start, start)
+    for stage, (others, own) in enumerate(zip(planes, (spot, line))):
+        row = jnp.broadcast_to(norm, (1, width))
+        count = len(others)
+        norm_send[stage] = row
+        norms[stage, own] = row
+        for other in others:
+            pltpu.make_async_remote_copy(
+                src_ref=norm_send.at[stage], dst_ref=norms.at[stage, own],
+                send_sem=norm_send_sem.at[stage], recv_sem=norm_recv_sem.at[stage],
+                device_id={"sector": other}, device_id_type=MESH,
+            ).start()
+        came = norms.at[stage, pl.ds(0, count)]
+        pltpu.make_async_copy(came, came, norm_recv_sem.at[stage]).wait()
+        norm = jnp.sum(norms[stage, 0:count + 1], axis=0)[:, 0:1]
+        pltpu.make_async_copy(came, came, norm_send_sem.at[stage]).wait()
+    norm = norm / cells
     for n in range(4):
         start_copy(n).start()
-    pltpu.make_async_copy(start_ref, zown, start_sem).wait()
-    start = zown[...]
-    send_rows([inner(start, start)], 1)
     for n in range(4):
         start_copy(n).wait()
-    (norm,) = wait_rows(1, 1)
-    wait_rows_sent(1)
     scale = lax.rsqrt(norm + EPS)
     xx_start = norm / (norm + EPS)
     pieces = []
     for j in range(nsrc):
         block = (start if j == 0 else start_halo[places[j - 1]]) * scale
-        ts[j] = block
-        xs[j] = jnp.zeros((width, width), F32)
-        ys[j] = jnp.zeros((width, width), F32)
+        if j == 0:
+            ts[...] = block
         pieces.append((block * alive[j]).astype(BF16))
-
-    def share(z, slot, halo):
-        zown[...] = z
-        if halo:
-            zsend[slot] = z.astype(HALO)
+    for ref in (xs, ys, us):
+        ref[...] = nothing
+
+    def share(slot, halo):
+        z = zs[...]
+        zsend[slot] = z.astype(HALO)
+
+        @pl.when(halo)
+        def _():
             for n in range(4):
                 halo_copy(n, slot).start()
-        send_rows([inner(xs[0], z), inner(ts[0], z), inner(ys[0], z), inner(z, z)], slot)
+
+        send_rows([inner(xs[...], z), inner(ts[...], z), inner(ys[...], z), inner(z, z)], slot)
 
     def rotate(slot, first, a, xx, yy, tt, inv):
         xz, tz, yz, zz = wait_rows(slot, 4)
@@ -300,47 +316,49 @@
         new_inv = lax.rsqrt(rho + EPS)
         return energy, cosine, sine, new_a, new_xx, new_yy, rho / (rho + EPS), new_inv
 
-    share(shared_multiply(0, pieces), 0, True)
-
-    def round_of(slot, first, carry, apply):
+    zs[...] = shared_multiply(0, nothing, pieces)
+    share(0, True)
+
+    def round_of(slot, first, last, carry, apply):
+        total = multiply(nothing, env, renv, [(0, zsend[slot])])
+        for n in range(4):
+            halo_copy(n, slot).wait_recv()
+        pieces = [None]
+        for j in range(1, nsrc):
+            pieces.append((zhalo[slot][places[j - 1]].astype(F32) * alive[j]).astype(BF16))
+        w = apply(total, pieces)
         a, xx, yy, tt, inv = carry
         _, cosine, sine, a, xx, yy, tt, inv = rotate(slot, first, a, xx, yy, tt, inv)
-        for n in range(4):
-            halo_copy(n, slot).wait_recv()
-        pieces = []
-        for j in range(nsrc):
-            z = zown[...] if j == 0 else zhalo[slot][places[j - 1]].astype(F32)
-            x = cosine * xs[j] + sine * ts[j]
-            y = cosine * ys[j] + sine * z
-            t = (y - a * x) * inv
-            xs[j] = x
-            ys[j] = y
-            ts[j] = t
-            pieces.append((t * alive[j]).astype(BF16))
-        z = apply(pieces)
+        x = cosine * xs[...] + sine * ts[...]
+        y = cosine * ys[...] + sine * zs[...]
+        u = cosine * us[...] + sine * w
+        xs[...] = x
+        ys[...] = y
+        us[...] = u
+        ts[...] = (y - a * x) * inv
+        zs[...] = (u - a * y) * inv
         for n in range(4):
             halo_copy(n, slot).wait_send()
         wait_rows_sent(slot)
-        share(z, 1 - slot, True)
+        share(1 - slot, jnp.logical_not(last))
         return a, xx, yy, tt, inv
 
     zero = jnp.zeros((1, 1), F32)
     carry = (zero, zero, zero, xx_start, zero + 1.0)
-    carry = round_of(0, True, carry, lambda pieces: shared_multiply(1, pieces))
-    carry = round_of(1, False, carry, lambda pieces: local_multiply(pieces, True))
-
-    def two_rounds(_, carry):
+    carry = round_of(0, True, False, carry, lambda total, pieces: shared_multiply(1, total, pieces))
+    carry = round_of(1, False, False, carry, lambda total, pieces: local_multiply(total, pieces, True))
+
+    def two_rounds(k, carry):
         for slot in range(2):
-            carry = round_of(slot, False, carry, lambda pieces: local_multiply(pieces, False))
+            last = jnp.logical_and(slot == 1, k == ITERS // 2 - 2)
+            carry = round_of(slot, False, last, carry, lambda total, pieces: local_multiply(total, pieces, False))
         return carry
 
     carry = lax.fori_loop(0, ITERS // 2 - 1, two_rounds, carry)
     slot = ITERS % 2
     energy, cosine, sine, *_ = rotate(slot, False, *carry)
-    state_ref[...] = cosine * xs[0] + sine * ts[0]
+    state_ref[...] = cosine * xs[...] + sine * ts[...]
     energy_ref[0] = energy[0, 0]
-    for n in range(4):
-        halo_copy(n, slot).wait()
     wait_rows_sent(slot)
 
     @pl.when(jnp.logical_not(last_site))
@@ -381,9 +399,10 @@
             pltpu.VMEM(flat, BF16),
             pltpu.VMEM((2, *flat[1:]), BF16),
             pltpu.VMEM((2, *flat[1:]), BF16),
-            pltpu.VMEM((nsrc, width, width), F32),
-            pltpu.VMEM((nsrc, width, width), F32),
-            pltpu.VMEM((nsrc, width, width), F32),
+            pltpu.VMEM((width, width), F32),
+            pltpu.VMEM((width, width), F32),
+            pltpu.VMEM((width, width), F32),
+            pltpu.VMEM((width, width), F32),
             pltpu.VMEM((width, width), F32),
             pltpu.VMEM((4, width, width), F32),
             pltpu.VMEM((2, width, width), HALO),
@@ -391,12 +410,14 @@
             pltpu.VMEM((4, width, width), HALO),
             pltpu.VMEM((2, 1, width), F32),
             pltpu.VMEM((2, blocks, 1, width), F32),
+            pltpu.VMEM((2, 1, width), F32),
+            pltpu.VMEM((2, 2 * GRID, 1, width), F32),
             pltpu.VMEM((2, 2, width, width), BF16),
             pltpu.VMEM((2, 2, width, width), BF16),
             pltpu.VMEM((2, width, width), PART),
             pltpu.VMEM((2, width, width), PART),
             dma((count,)), dma((count,)), dma((count,)), dma, dma((4,)), dma((4,)),
-            dma((2, 4)), dma((2, 4)), dma((2,)), dma((2,)),
+            dma((2, 4)), dma((2, 4)), dma((2,)), dma((2,)), dma((2,)), dma((2,)),
             dma, dma((count // 2,)), dma((count // 2,)), dma((2,)), dma((2,)), dma((2,)), dma((2,)),
         ],
         compiler_params=pltpu.CompilerParams(

time: 102 us -> 97.6 us (0.957)
  Pallas kernels: 96.7 us -> 92.9 us
    pallas_call x1, Pallas kernels: 96.7 us -> 92.9 us  [per_device(): pl.pallas_call(body, out_shape=(jax.ShapeDtypeStruct((width, width), F32)...]
where the time goes in v3:
time: 97.6 us; the launch traced here: 97.4 us
  Pallas kernels  92.9 us (95%)
  between operations  3.03 us (3%)
  local copies, waits for them, and re-layouts  1.47 us (2%)
    pallas_call x1, Pallas kernels, per_device(): pl.pallas_call(body, out_shape=(jax.ShapeDtypeStruct((width, width), F32)...  92.9 us

profile of v3, /device:TPU:128, one launch (start us, length us, event | category | flops | bytes accessed | tf_op | source)
XLA Modules:
  0.0 97.4 jit_solution(15880573306274075424)
XLA Ops:
  1.3 92.9 %window.1 = (f32[128,128]{1,0:T(8,128)}, f32[1]{0:T(128)}) custom-call(f32[128,128]{1,0:T(8,128)} %bitcast.12, bf16[4,1536,128]{2,1,0:T(8,128)(2,1)} %bitcast.8, bf16[4,1536,128]{2,1,0:T(8,128)(2,1)} %bitcast.9, bf16[4,1536,128]{2,1,0:T(8,128)(2,1)} %bitcast.10, s32[4]{0:T(128)} %bitcast.13, s32[1]{0:T(128)} %bitcast.7.live_ref), custom_call_target="tpu_custom_call" | custom-call | tf_op jit(solution)/shard_map/window/pallas_call | solution.py:389
  94.2 1.5 %copy.11 = f32[1,1,128,128]{3,2,1,0:T(8,128)} copy(f32[1,1,128,128]{3,2,1,0:T(8,128)} %bitcast.11) | data formatting | bytes 131072

commit v4 on v3

--- a/solution.py
+++ b/solution.py
@@ -9,8 +9,8 @@
 
 GRID = 4
 ITERS = 8
-GROUP = 3
-LATE_FIRST = 3
+GROUP = 2
+LATE_FIRST = 4
 HALO = jnp.bfloat16
 PART = jnp.bfloat16
 EPS = 1e-06
@@ -239,13 +239,15 @@
 
         return total + part_in[n].astype(F32)
 
-    def local_multiply(total, pieces, wait):
+    def local_multiply(total, pieces, sums, wait):
         if wait:
             @pl.when(jnp.logical_not(first_site))
             def _():
                 for i in late:
                     wait_env(i)
-        return multiply(total, env, renv, [(j, pieces[j]) for j in range(1, nsrc)])
+        total = multiply(total, env, renv, [(1, pieces[1])])
+        turned = sums()
+        return multiply(total, env, renv, [(j, pieces[j]) for j in range(2, nsrc)]), turned
 
     pltpu.make_async_copy(start_ref, zs, start_sem).wait()
     start = zs[...]
@@ -281,16 +283,16 @@
     for ref in (xs, ys, us):
         ref[...] = nothing
 
-    def share(slot, halo):
-        z = zs[...]
+    def share_halo(z, slot, halo):
         zsend[slot] = z.astype(HALO)
 
         @pl.when(halo)
         def _():
-            for n in range(4):
+            for n in (2, 3, 0, 1):
                 halo_copy(n, slot).start()
 
-        send_rows([inner(xs[...], z), inner(ts[...], z), inner(ys[...], z), inner(z, z)], slot)
+    def share_sums(x, t, y, z, slot):
+        send_rows([inner(x, z), inner(t, z), inner(y, z), inner(z, z)], slot)
 
     def rotate(slot, first, a, xx, yy, tt, inv):
         xz, tz, yz, zz = wait_rows(slot, 4)
@@ -316,8 +318,10 @@
         new_inv = lax.rsqrt(rho + EPS)
         return energy, cosine, sine, new_a, new_xx, new_yy, rho / (rho + EPS), new_inv
 
-    zs[...] = shared_multiply(0, nothing, pieces)
-    share(0, True)
+    image = shared_multiply(0, nothing, pieces)
+    zs[...] = image
+    share_halo(image, 0, True)
+    share_sums(xs[...], ts[...], ys[...], image, 0)
 
     def round_of(slot, first, last, carry, apply):
         total = multiply(nothing, env, renv, [(0, zsend[slot])])
@@ -326,32 +330,34 @@
         pieces = [None]
         for j in range(1, nsrc):
             pieces.append((zhalo[slot][places[j - 1]].astype(F32) * alive[j]).astype(BF16))
-        w = apply(total, pieces)
-        a, xx, yy, tt, inv = carry
-        _, cosine, sine, a, xx, yy, tt, inv = rotate(slot, first, a, xx, yy, tt, inv)
-        x = cosine * xs[...] + sine * ts[...]
+        w, turned = apply(total, pieces, lambda: rotate(slot, first, *carry))
+        _, cosine, sine, a, xx, yy, tt, inv = turned
         y = cosine * ys[...] + sine * zs[...]
         u = cosine * us[...] + sine * w
+        z = (u - a * y) * inv
+        share_halo(z, 1 - slot, jnp.logical_not(last))
+        x = cosine * xs[...] + sine * ts[...]
+        t = (y - a * x) * inv
+        share_sums(x, t, y, z, 1 - slot)
         xs[...] = x
         ys[...] = y
         us[...] = u
-        ts[...] = (y - a * x) * inv
-        zs[...] = (u - a * y) * inv
+        ts[...] = t
+        zs[...] = z
         for n in range(4):
             halo_copy(n, slot).wait_send()
         wait_rows_sent(slot)
-        share(1 - slot, jnp.logical_not(last))
         return a, xx, yy, tt, inv
 
     zero = jnp.zeros((1, 1), F32)
     carry = (zero, zero, zero, xx_start, zero + 1.0)
-    carry = round_of(0, True, False, carry, lambda total, pieces: shared_multiply(1, total, pieces))
-    carry = round_of(1, False, False, carry, lambda total, pieces: local_multiply(total, pieces, True))
+    carry = round_of(0, True, False, carry, lambda total, pieces, sums: (shared_multiply(1, total, pieces), sums()))
+    carry = round_of(1, False, False, carry, lambda total, pieces, sums: local_multiply(total, pieces, sums, True))
 
     def two_rounds(k, carry):
         for slot in range(2):
             last = jnp.logical_and(slot == 1, k == ITERS // 2 - 2)
-            carry = round_of(slot, False, last, carry, lambda total, pieces: local_multiply(total, pieces, False))
+            carry = round_of(slot, False, last, carry, lambda total, pieces, sums: local_multiply(total, pieces, sums, False))
         return carry
 
     carry = lax.fori_loop(0, ITERS // 2 - 1, two_rounds, carry)

time: 97.6 us -> 96.4 us (0.988)
  Pallas kernels: 92.9 us -> 91.7 us
    pallas_call x1, Pallas kernels: 92.9 us -> 91.7 us  [per_device(): pl.pallas_call(body, out_shape=(jax.ShapeDtypeStruct((width, width), F32)...]
where the time goes in v4:
time: 96.4 us; the launch traced here: 96.2 us
  Pallas kernels  91.7 us (95%)
  between operations  3.03 us (3%)
  local copies, waits for them, and re-layouts  1.47 us (2%)
    pallas_call x1, Pallas kernels, per_device(): pl.pallas_call(body, out_shape=(jax.ShapeDtypeStruct((width, width), F32)...  91.7 us

profile of v4, /device:TPU:128, one launch (start us, length us, event | category | flops | bytes accessed | tf_op | source)
XLA Modules:
  0.0 96.2 jit_solution(9563509961625448309)
XLA Ops:
  1.3 91.7 %window.1 = (f32[128,128]{1,0:T(8,128)}, f32[1]{0:T(128)}) custom-call(f32[128,128]{1,0:T(8,128)} %bitcast.12, bf16[4,1536,128]{2,1,0:T(8,128)(2,1)} %bitcast.8, bf16[4,1536,128]{2,1,0:T(8,128)(2,1)} %bitcast.9, bf16[4,1536,128]{2,1,0:T(8,128)(2,1)} %bitcast.10, s32[4]{0:T(128)} %bitcast.13, s32[1]{0:T(128)} %bitcast.7.live_ref), custom_call_target="tpu_custom_call" | custom-call | tf_op jit(solution)/shard_map/window/pallas_call | solution.py:395
  93.0 1.5 %copy.11 = f32[1,1,128,128]{3,2,1,0:T(8,128)} copy(f32[1,1,128,128]{3,2,1,0:T(8,128)} %bitcast.11) | data formatting | bytes 131072

commit v5 on v4

--- a/solution.py
+++ b/solution.py
@@ -24,10 +24,11 @@
     start_ref, left_ref, edge_ref, right_ref, ids_ref, live_ref,
     state_ref, energy_ref,
     env, renv, help_env, help_renv, xs, ys, us, ts, zs, start_halo, zsend, zhalo_even, zhalo_odd, row_send, rows, norm_send, norms,
-    piece_send, piece_in, part_send, part_in,
+    piece_send, piece_in, part_send, part_in, facts_send, facts_in, help_halo,
     env_send, env_recv, renv_sem, start_sem, start_send, start_recv,
     halo_send, halo_recv, row_send_sem, row_recv_sem, norm_send_sem, norm_recv_sem,
     help_env_sem, help_renv_send, help_renv_recv, piece_sends, piece_recvs, part_sends, part_recvs,
+    facts_sems, help_sends, help_recvs,
 ):
     site = lax.axis_index("site")
     me = lax.axis_index("sector")
@@ -77,6 +78,8 @@
         barrier, len(planes[0]) + len(planes[1]) + jnp.where(site > 0, 1, 0) + jnp.where(site < sites - 1, 1, 0)
     )
 
+    hops = (1, -1, GRID, -GRID)
+
     def env_copy(i):
         p, g = steps[i]
         return pltpu.make_async_remote_copy(
@@ -92,6 +95,19 @@
             device_id={"site": site - 1}, device_id_type=MESH,
         )
 
+    def facts_copy():
+        return pltpu.make_async_remote_copy(
+            src_ref=facts_send, dst_ref=facts_in, send_sem=facts_sems.at[0], recv_sem=facts_sems.at[1],
+            device_id={"site": site - 1}, device_id_type=MESH,
+        )
+
+    def help_halo_copy(n):
+        return pltpu.make_async_remote_copy(
+            src_ref=zsend.at[0], dst_ref=help_halo.at[n],
+            send_sem=help_sends.at[n], recv_sem=help_recvs.at[n],
+            device_id={"site": site - 1, "sector": peer(hops[n])}, device_id_type=MESH,
+        )
+
     def piece_copy(n):
         return pltpu.make_async_remote_copy(
             src_ref=piece_send.at[n], dst_ref=piece_in.at[n],
@@ -111,12 +127,18 @@
         for i in early:
             env_copy(i).start()
 
+    lane = lax.broadcasted_iota(jnp.int32, (1, width), 1)
+    facts = jnp.where(lane == 0, live_ref[0, 0], 0)
+    for j in range(1, nsrc):
+        facts = jnp.where(lane == j, ids_ref[0, 0, j], facts)
+    facts_send[...] = facts
+
     @pl.when(jnp.logical_not(first_site))
     def _():
+        facts_copy().start()
         for g in range(groups - 1):
             help_copy(g).start()
 
-    hops = (1, -1, GRID, -GRID)
     zhalo = (zhalo_even, zhalo_odd)
 
     def start_copy(n):
@@ -164,11 +186,12 @@
     def inner(a, b):
         return jnp.sum(jnp.sum(a * b, axis=0, keepdims=True), axis=1, keepdims=True)
 
-    places = []
-    for j in range(1, nsrc):
-        offset = ids_ref[j] - me
-        places.append(jnp.where(offset == -1, 0, jnp.where(offset == 1, 1, jnp.where(offset == -GRID, 2, 3))))
-    alive = [(j < live_ref[0]).astype(F32) for j in range(nsrc)]
+    def place_of(source):
+        offset = source - me
+        return jnp.where(offset == -1, 0, jnp.where(offset == 1, 1, jnp.where(offset == -GRID, 2, 3)))
+
+    places = [place_of(ids_ref[0, 0, j]) for j in range(1, nsrc)]
+    alive = [(j < live_ref[0, 0]).astype(F32) for j in range(nsrc)]
 
     def multiply(total, e_ref, r_ref, jobs, wait=None):
         size = GROUP if wait else terms
@@ -189,22 +212,31 @@
 
     nothing = jnp.zeros((width, width), F32)
 
-    def shared_multiply(n, total, pieces):
-        piece_send[n, 0] = pieces[2]
-        piece_send[n, 1] = pieces[3]
-
-        @pl.when(jnp.logical_not(first_site))
-        def _():
-            piece_copy(n).start()
-            if n == 0:
+    def shared_multiply(n, total, pieces, sums):
+        if n == 0:
+            piece_send[0, 0] = pieces[2]
+            piece_send[0, 1] = pieces[3]
+
+            @pl.when(jnp.logical_not(first_site))
+            def _():
+                piece_copy(0).start()
                 help_copy(groups - 1).start()
 
         @pl.when(jnp.logical_not(last_site))
         def _():
-            piece = pltpu.make_async_copy(piece_in.at[n], piece_in.at[n], piece_recvs.at[n])
-            piece.wait()
             if n == 0:
+                pltpu.make_async_copy(piece_in.at[0], piece_in.at[0], piece_recvs.at[0]).wait()
                 pltpu.make_async_copy(help_env, help_env, help_env_sem).wait()
+                pltpu.make_async_copy(facts_in, facts_in, facts_sems.at[1]).wait()
+                two = [piece_in[0, 0], piece_in[0, 1]]
+            else:
+                for m in range(4):
+                    pltpu.make_async_copy(help_halo.at[m], help_halo.at[m], help_recvs.at[m]).wait()
+                facts = facts_in[...]
+                two = []
+                for j in range(2, nsrc):
+                    piece = help_halo[place_of(facts[0, j])].astype(F32)
+                    two.append((piece * (j < facts[0, 0]).astype(F32)).astype(BF16))
 
             def arrived(g):
                 pltpu.make_async_copy(
@@ -212,7 +244,7 @@
                 ).wait()
 
             part_send[n] = multiply(
-                nothing, help_env, help_renv, [(0, piece_in[n, 0]), (1, piece_in[n, 1])], None if n else arrived
+                nothing, help_env, help_renv, [(0, two[0]), (1, two[1])], None if n else arrived
             ).astype(PART)
             part_copy(n).start()
             for i in (late[:LATE_FIRST], late[LATE_FIRST:])[n]:
@@ -225,6 +257,7 @@
             total = multiply(total, env, renv, [(0, pieces[0]), (1, pieces[1])], lambda g: wait_env(early[g]))
         else:
             total = multiply(total, env, renv, [(1, pieces[1])])
+        turned = sums()
 
         @pl.when(first_site)
         def _():
@@ -237,7 +270,7 @@
         def _():
             pltpu.make_async_copy(part_in.at[n], part_in.at[n], part_recvs.at[n]).wait()
 
-        return total + part_in[n].astype(F32)
+        return total + part_in[n].astype(F32), turned
 
     def local_multiply(total, pieces, sums, wait):
         if wait:
@@ -318,9 +351,15 @@
         new_inv = lax.rsqrt(rho + EPS)
         return energy, cosine, sine, new_a, new_xx, new_yy, rho / (rho + EPS), new_inv
 
-    image = shared_multiply(0, nothing, pieces)
+    image, _ = shared_multiply(0, nothing, pieces, lambda: None)
     zs[...] = image
     share_halo(image, 0, True)
+
+    @pl.when(jnp.logical_not(first_site))
+    def _():
+        for n in (2, 3, 0, 1):
+            help_halo_copy(n).start()
+
     share_sums(xs[...], ts[...], ys[...], image, 0)
 
     def round_of(slot, first, last, carry, apply):
@@ -347,11 +386,17 @@
         for n in range(4):
             halo_copy(n, slot).wait_send()
         wait_rows_sent(slot)
+        if first:
+            @pl.when(jnp.logical_not(first_site))
+            def _():
+                for n in range(4):
+                    help_halo_copy(n).wait_send()
+
         return a, xx, yy, tt, inv
 
     zero = jnp.zeros((1, 1), F32)
     carry = (zero, zero, zero, xx_start, zero + 1.0)
-    carry = round_of(0, True, False, carry, lambda total, pieces, sums: (shared_multiply(1, total, pieces), sums()))
+    carry = round_of(0, True, False, carry, lambda total, pieces, sums: shared_multiply(1, total, pieces, sums))
     carry = round_of(1, False, False, carry, lambda total, pieces, sums: local_multiply(total, pieces, sums, True))
 
     def two_rounds(k, carry):
@@ -378,8 +423,8 @@
     def _():
         for g in range(groups):
             help_copy(g).wait_send()
-        for n in range(2):
-            piece_copy(n).wait_send()
+        piece_copy(0).wait_send()
+        facts_copy().wait_send()
 
 
 def per_device(initial_state, left_env, edge_env, right_env, source_blocks, live_terms):
@@ -418,13 +463,17 @@
             pltpu.VMEM((2, blocks, 1, width), F32),
             pltpu.VMEM((2, 1, width), F32),
             pltpu.VMEM((2, 2 * GRID, 1, width), F32),
-            pltpu.VMEM((2, 2, width, width), BF16),
-            pltpu.VMEM((2, 2, width, width), BF16),
+            pltpu.VMEM((1, 2, width, width), BF16),
+            pltpu.VMEM((1, 2, width, width), BF16),
             pltpu.VMEM((2, width, width), PART),
             pltpu.VMEM((2, width, width), PART),
+            pltpu.VMEM((1, width), jnp.int32),
+            pltpu.VMEM((1, width), jnp.int32),
+            pltpu.VMEM((4, width, width), HALO),
             dma((count,)), dma((count,)), dma((count,)), dma, dma((4,)), dma((4,)),
             dma((2, 4)), dma((2, 4)), dma((2,)), dma((2,)), dma((2,)), dma((2,)),
             dma, dma((count // 2,)), dma((count // 2,)), dma((2,)), dma((2,)), dma((2,)), dma((2,)),
+            dma((2,)), dma((4,)), dma((4,)),
         ],
         compiler_params=pltpu.CompilerParams(
             collective_id=0, has_side_effects=True, vmem_limit_bytes=60 * 1024 * 1024
@@ -435,8 +484,8 @@
         left_env.reshape(flat),
         edge_env.reshape(flat),
         right_env.reshape(flat),
-        source_blocks.reshape(nsrc),
-        live_terms.reshape(1),
+        source_blocks,
+        live_terms,
     )
     return state[None, None], energy
 

time: 96.4 us -> 95.4 us (0.990)
  no operation moved by 1% of the time
where the time goes in v5:
time: 95.4 us; the launch traced here: 95.3 us
  Pallas kernels  90.8 us (95%)
  between operations  3.03 us (3%)
  local copies, waits for them, and re-layouts  1.47 us (2%)
    pallas_call x1, Pallas kernels, per_device(): pl.pallas_call(body, out_shape=(jax.ShapeDtypeStruct((width, width), F32)...  90.8 us

profile of v5, /device:TPU:128, one launch (start us, length us, event | category | flops | bytes accessed | tf_op | source)
XLA Modules:
  0.0 95.3 jit_solution(2789940876235462869)
XLA Ops:
  1.3 90.8 %window.1 = (f32[128,128]{1,0:T(8,128)}, f32[1]{0:T(128)}) custom-call(f32[128,128]{1,0:T(8,128)} %bitcast.9, bf16[4,1536,128]{2,1,0:T(8,128)(2,1)} %bitcast.5, bf16[4,1536,128]{2,1,0:T(8,128)(2,1)} %bitcast.6, bf16[4,1536,128]{2,1,0:T(8,128)(2,1)} %bitcast.7, s32[1,1,4]{2,1,0:T(1,128)} %ids_ref.1, s32[1,1]{1,0:T(1,128)S(6)} %copy.10.live_ref), custom_call_target="tpu_custom_call" | custom-call | tf_op jit(solution)/shard_map/window/pallas_call | solution.py:440
  92.0 1.5 %copy.11 = f32[1,1,128,128]{3,2,1,0:T(8,128)} copy(f32[1,1,128,128]{3,2,1,0:T(8,128)} %bitcast.8) | data formatting | bytes 131072

commit v6 on v5

--- a/solution.py
+++ b/solution.py
@@ -53,9 +53,14 @@
         pl.semaphore_signal(barrier, inc=1, device_id={"site": site + 1}, device_id_type=MESH)
 
     side = 2 * GRID
-    base, spot, line = me - lax.rem(me, side), lax.rem(me, side), me // side
-    planes = ([base + lax.rem(spot + d, side) for d in range(1, side)], [peer(d) for d in range(side, blocks, side)])
-    for other in planes[0] + planes[1]:
+    spot, base = lax.rem(me, side), me - lax.rem(me, side)
+    planes = (
+        [me + 1 - 2 * lax.rem(me, 2)],
+        [base + lax.rem(spot + d, side) for d in range(2, side, 2)],
+        [peer(d) for d in range(side, blocks, side)],
+    )
+    owns = (lax.rem(me, 2), spot // 2, me // side)
+    for other in planes[0] + planes[1] + planes[2]:
         pl.semaphore_signal(barrier, inc=1, device_id={"sector": other}, device_id_type=MESH)
 
     def span(ref, p, g):
@@ -75,7 +80,7 @@
         pltpu.make_async_copy(left_ref.at[pl.ds(2, 2)], help_env, help_env_sem).start()
 
     pl.semaphore_wait(
-        barrier, len(planes[0]) + len(planes[1]) + jnp.where(site > 0, 1, 0) + jnp.where(site < sites - 1, 1, 0)
+        barrier, sum(len(plane) for plane in planes) + jnp.where(site > 0, 1, 0) + jnp.where(site < sites - 1, 1, 0)
     )
 
     hops = (1, -1, GRID, -GRID)
@@ -285,7 +290,7 @@
     pltpu.make_async_copy(start_ref, zs, start_sem).wait()
     start = zs[...]
     norm = inner(start, start)
-    for stage, (others, own) in enumerate(zip(planes, (spot, line))):
+    for stage, (others, own) in enumerate(zip(planes, owns)):
         row = jnp.broadcast_to(norm, (1, width))
         count = len(others)
         norm_send[stage] = row
@@ -461,8 +466,8 @@
             pltpu.VMEM((4, width, width), HALO),
             pltpu.VMEM((2, 1, width), F32),
             pltpu.VMEM((2, blocks, 1, width), F32),
-            pltpu.VMEM((2, 1, width), F32),
-            pltpu.VMEM((2, 2 * GRID, 1, width), F32),
+            pltpu.VMEM((3, 1, width), F32),
+            pltpu.VMEM((3, GRID, 1, width), F32),
             pltpu.VMEM((1, 2, width, width), BF16),
             pltpu.VMEM((1, 2, width, width), BF16),
             pltpu.VMEM((2, width, width), PART),
@@ -471,7 +476,7 @@
             pltpu.VMEM((1, width), jnp.int32),
             pltpu.VMEM((4, width, width), HALO),
             dma((count,)), dma((count,)), dma((count,)), dma, dma((4,)), dma((4,)),
-            dma((2, 4)), dma((2, 4)), dma((2,)), dma((2,)), dma((2,)), dma((2,)),
+            dma((2, 4)), dma((2, 4)), dma((2,)), dma((2,)), dma((3,)), dma((3,)),
             dma, dma((count // 2,)), dma((count // 2,)), dma((2,)), dma((2,)), dma((2,)), dma((2,)),
             dma((2,)), dma((4,)), dma((4,)),
         ],

time: 95.4 us -> 94.5 us (level)
  Pallas kernels: 90.8 us -> 89.8 us
    pallas_call x1, Pallas kernels: 90.8 us -> 89.8 us  [per_device(): pl.pallas_call(body, out_shape=(jax.ShapeDtypeStruct((width, width), F32)...]
where the time goes in v6:
time: 94.5 us; the launch traced here: 94.3 us
  Pallas kernels  89.8 us (95%)
  between operations  3.03 us (3%)
  local copies, waits for them, and re-layouts  1.47 us (2%)
    pallas_call x1, Pallas kernels, per_device(): pl.pallas_call(body, out_shape=(jax.ShapeDtypeStruct((width, width), F32)...  89.8 us

profile of v6, /device:TPU:128, one launch (start us, length us, event | category | flops | bytes accessed | tf_op | source)
XLA Modules:
  0.0 94.3 jit_solution(16584445697407300762)
XLA Ops:
  1.3 89.8 %window.1 = (f32[128,128]{1,0:T(8,128)}, f32[1]{0:T(128)}) custom-call(f32[128,128]{1,0:T(8,128)} %bitcast.9, bf16[4,1536,128]{2,1,0:T(8,128)(2,1)} %bitcast.5, bf16[4,1536,128]{2,1,0:T(8,128)(2,1)} %bitcast.6, bf16[4,1536,128]{2,1,0:T(8,128)(2,1)} %bitcast.7, s32[1,1,4]{2,1,0:T(1,128)} %ids_ref.1, s32[1,1]{1,0:T(1,128)S(6)} %copy.10.live_ref), custom_call_target="tpu_custom_call" | custom-call | tf_op jit(solution)/shard_map/window/pallas_call | solution.py:445
  91.1 1.5 %copy.11 = f32[1,1,128,128]{3,2,1,0:T(8,128)} copy(f32[1,1,128,128]{3,2,1,0:T(8,128)} %bitcast.8) | data formatting | bytes 131072
